TPU v7x, 32 devices: a whole 2x2x4 slice. The times are simulated.
32 devices in a mesh: grp: 4 (over z), seq: 8 (over y, x, core).
Axes of the slice: x: 2, y: 2, z: 4, core: 2. Of those that a mesh axis runs over, the one named last changes fastest.
Arguments:
- query: bfloat16 [4096, 1024], P(('grp', 'seq')), may hold values from -6 to 6
- keys: bfloat16 [4096, 1024], P(('grp', 'seq')), may hold values from -6 to 6
- values: bfloat16 [4096, 1024], P(('grp', 'seq')), may hold values from -6 to 6
- d_out: bfloat16 [4096, 1024], P(('grp', 'seq')), may hold values from -6 to 6
- rand_blocks: int32 [32, 3], replicated, may hold values from 0 to 31, as said below
- global_blocks: int32 [2], replicated, may hold values from 0 to 31, as said below
Outputs:
- attended: bfloat16 [4096, 1024], P(('grp', 'seq'))
- d_query: bfloat16 [4096, 1024], P(('grp', 'seq'))
- d_keys: bfloat16 [4096, 1024], P(('grp', 'seq'))
- d_values: bfloat16 [4096, 1024], P(('grp', 'seq'))
Inputs may be any that keep to these rules, and one draw needn't show every extreme that they name: `rand_blocks`: the 3 entries of row b are distinct; each lies in another segment than b and in the same column: (r) % 8 equals (b) % 8 and r // 8 differs from b // 8. `global_blocks`: the 2 entries are distinct; one of them is the last block.
All inputs are finite; a program needn't handle non-finite values.
Results may differ from a plain program's by a relative error of at most 0.0074.
Values may be sent and summed in bfloat16 or wider, within the bound.
A program may use at most 128 MiB of HBM per device.

v0:
```python
import functools
import math

import jax
import jax.numpy as jnp
from jax import lax
from jax.experimental import pallas as pl
from jax.experimental.pallas import tpu as pltpu
from jax.sharding import PartitionSpec as P

HEAD_DIM = 64
BLOCK = 128
GLOBALS = 2
RANDOMS = 3
KEYS = 8


def extended(block, sides, width, periodic):
    for axis, dim in sides:
        count = lax.axis_size(axis)
        forward = [(i, i + 1) for i in range(count - 1)]
        if periodic:
            forward.append((count - 1, 0))
        backward = [(target, source) for source, target in forward]
        low = lax.ppermute(
            lax.slice_in_dim(block, block.shape[dim] - width, None, axis=dim), axis, forward
        )
        high = lax.ppermute(lax.slice_in_dim(block, 0, width, axis=dim), axis, backward)
        block = jnp.concatenate([low, block, high], axis=dim)
    return block


def broadcast(block, axis, source):
    block = jnp.where(lax.axis_index(axis) == source, block, jnp.zeros_like(block))
    return lax.psum(block, axis)


def attend_blocks(queries, key_rows, value_rows, grad_rows, key_valid):
    factor = 1.0 / math.sqrt(queries.shape[-1])
    scores = (
        jnp.einsum("nqhe,njkhe->nhqjk", queries, key_rows, preferred_element_type=jnp.float32)
        * factor
    )
    scores = jnp.where(key_valid[:, None, None, :, None], scores, -1e30)
    row_max = jnp.max(scores, axis=(3, 4), keepdims=True)
    raised = jnp.exp(scores - row_max)
    attn_prob = raised / jnp.sum(raised, axis=(3, 4), keepdims=True)
    prob_half = attn_prob.astype(jnp.bfloat16)
    result = jnp.einsum(
        "nhqjk,njkhe->nqhe", prob_half, value_rows, preferred_element_type=jnp.float32
    )
    d_prob = jnp.einsum(
        "nqhe,njkhe->nhqjk", grad_rows, value_rows, preferred_element_type=jnp.float32
    )
    row_dot = jnp.sum(attn_prob * d_prob, axis=(3, 4), keepdims=True)
    d_scores = (attn_prob * (d_prob - row_dot) * factor).astype(jnp.bfloat16)
    d_query = jnp.einsum(
        "nhqjk,njkhe->nqhe", d_scores, key_rows, preferred_element_type=jnp.float32
    )
    d_keys = jnp.einsum("nhqjk,nqhe->njkhe", d_scores, queries, preferred_element_type=jnp.float32)
    d_values = jnp.einsum(
        "nhqjk,nqhe->njkhe", prob_half, grad_rows, preferred_element_type=jnp.float32
    )
    return (result, d_query, d_keys, d_values)


def body(query, keys, values, d_out, rand_blocks, global_blocks):
    group_count = lax.axis_size("grp")
    column_count = lax.axis_size("seq")
    column = lax.axis_index("seq")
    tokens_dev = query.shape[0]
    width = query.shape[1]
    local_blocks = tokens_dev // BLOCK
    head_width = width // group_count
    heads_here = head_width // HEAD_DIM
    block_total = group_count * column_count * local_blocks
    segment_span = column_count * local_blocks
    stride = local_blocks + 2
    count = group_count * local_blocks
    per_step = 4
    steps_count = count // per_step
    stacked = jnp.stack([keys, values])
    widened = extended(stacked, ((("grp", "seq"), 1),), BLOCK, False)
    key_send = widened[0][None]
    value_send = widened[1][None]
    query_heads, grad_heads, key_heads, value_heads = (
        lax.all_to_all(
            query.reshape(1, tokens_dev, width), "grp", split_axis=2, concat_axis=0, tiled=True
        ),
        lax.all_to_all(
            d_out.reshape(1, tokens_dev, width), "grp", split_axis=2, concat_axis=0, tiled=True
        ),
        lax.all_to_all(key_send, "grp", split_axis=2, concat_axis=0, tiled=True),
        lax.all_to_all(value_send, "grp", split_axis=2, concat_axis=0, tiled=True),
    )
    ext_pair = jnp.stack([key_heads, value_heads]).reshape(
        2, group_count * stride, BLOCK, head_width
    )
    global_device = global_blocks // local_blocks
    global_segment = global_device // column_count
    global_column = global_device % column_count
    global_local = global_blocks % local_blocks
    global_rows = global_segment * stride + global_local + 1
    fetched = []
    for which in range(GLOBALS):
        fetched.append(broadcast(ext_pair[:, global_rows[which]], "seq", global_column[which]))
    global_pair = jnp.stack(fetched, axis=1)
    segment_of = jnp.repeat(jnp.arange(group_count, dtype=jnp.int32), local_blocks)
    local_of = jnp.tile(jnp.arange(local_blocks, dtype=jnp.int32), group_count)
    query_ids = (segment_of * column_count + column) * local_blocks + local_of
    rand_ids = jnp.take(rand_blocks, query_ids, axis=0)
    rand_rows = rand_ids // segment_span * stride + rand_ids % local_blocks + 1
    window_rows = (segment_of * stride + local_of)[:, None] + jnp.arange(3, dtype=jnp.int32)[
        None, :
    ]
    key_table = jnp.concatenate([window_rows, rand_rows], axis=1)
    key_valid = jnp.concatenate(
        [
            (query_ids > 0)[:, None],
            jnp.ones((count, 1), dtype=jnp.bool_),
            (query_ids < block_total - 1)[:, None],
            jnp.ones((count, GLOBALS + RANDOMS), dtype=jnp.bool_),
        ],
        axis=1,
    )
    query_steps = query_heads.reshape(steps_count, per_step, BLOCK, heads_here, HEAD_DIM)
    grad_steps = grad_heads.reshape(steps_count, per_step, BLOCK, heads_here, HEAD_DIM)
    table_steps = key_table.reshape(steps_count, per_step, 3 + RANDOMS)
    valid_steps = key_valid.reshape(steps_count, per_step, KEYS)
    global_spread = jnp.broadcast_to(
        global_pair[:, None], (2, per_step, GLOBALS, BLOCK, head_width)
    )

    def advance(totals, packed):
        ext_total, global_total = totals
        query_part, grad_part, rows_part, valid_part = packed
        taken = jnp.stack(
            [
                lax.dynamic_index_in_dim(ext_pair, row, axis=1, keepdims=False)
                for row in rows_part.reshape(-1)
            ],
            axis=1,
        ).reshape(2, per_step, 3 + RANDOMS, BLOCK, head_width)
        gathered = jnp.concatenate([taken[:, :, :3], global_spread, taken[:, :, 3:]], axis=2)
        gathered = gathered.reshape(2, per_step, KEYS, BLOCK, heads_here, HEAD_DIM)
        result, d_query, d_keys, d_values = attend_blocks(
            query_part, gathered[0], gathered[1], grad_part, valid_part
        )
        d_pair = jnp.stack([d_keys, d_values]).reshape(2, per_step, KEYS, BLOCK, head_width)
        spread_back = jnp.concatenate([d_pair[:, :, :3], d_pair[:, :, 3 + GLOBALS :]], axis=2)
        spread_back = spread_back.reshape(2, per_step * (3 + RANDOMS), BLOCK, head_width)
        ext_total = ext_total.at[:, rows_part.reshape(-1)].add(spread_back)
        global_total = global_total + jnp.sum(d_pair[:, :, 3 : 3 + GLOBALS], axis=1)
        return (
            (ext_total, global_total),
            (result.astype(jnp.bfloat16), d_query.astype(jnp.bfloat16)),
        )

    start_totals = (
        jnp.zeros((2, group_count * stride, BLOCK, head_width), jnp.float32),
        jnp.zeros((2, GLOBALS, BLOCK, head_width), jnp.float32),
    )
    totals, outputs = lax.scan(
        advance, start_totals, (query_steps, grad_steps, table_steps, valid_steps)
    )
    ext_total = totals[0].reshape(2, group_count, stride, BLOCK, head_width)
    global_sum = lax.psum(totals[1], "seq")
    own_grad = ext_total[:, :, 1 : local_blocks + 1]
    for which in range(GLOBALS):
        addend = jnp.where(column == global_column[which], global_sum[:, which], 0.0)
        own_grad = own_grad.at[:, global_segment[which], global_local[which]].add(addend)
    send_left = ext_total[:, :, 0]
    send_right = ext_total[:, :, local_blocks + 1]
    empty_edge = jnp.zeros_like(send_left[:, :1])
    send_left = jnp.where(
        column == 0, jnp.concatenate([send_left[:, 1:], empty_edge], axis=1), send_left
    )
    send_right = jnp.where(
        column == column_count - 1,
        jnp.concatenate([empty_edge, send_right[:, :-1]], axis=1),
        send_right,
    )
    edges = jnp.concatenate([send_left, send_right], axis=2)
    arrived = extended(edges, (("seq", 2),), BLOCK, True)
    own_grad = own_grad.at[:, :, 0].add(arrived[:, :, :BLOCK])
    own_grad = own_grad.at[:, :, local_blocks - 1].add(arrived[:, :, 3 * BLOCK :])
    head_shape = (group_count, tokens_dev, head_width)
    attended_heads = outputs[0].reshape(head_shape)
    d_query_heads = outputs[1].reshape(head_shape)
    d_key_heads = own_grad[0].reshape(head_shape).astype(jnp.bfloat16)
    d_value_heads = own_grad[1].reshape(head_shape).astype(jnp.bfloat16)
    returned = (
        lax.all_to_all(attended_heads, "grp", split_axis=0, concat_axis=2, tiled=True),
        lax.all_to_all(d_query_heads, "grp", split_axis=0, concat_axis=2, tiled=True),
        lax.all_to_all(d_key_heads, "grp", split_axis=0, concat_axis=2, tiled=True),
        lax.all_to_all(d_value_heads, "grp", split_axis=0, concat_axis=2, tiled=True),
    )
    return (
        returned[0].reshape(tokens_dev, width),
        returned[1].reshape(tokens_dev, width),
        returned[2].reshape(tokens_dev, width),
        returned[3].reshape(tokens_dev, width),
    )


MESH = pl.DeviceIdType.MESH
F32 = jnp.float32
BF16 = jnp.bfloat16
LANES = 128


def contract(left, right, dims):
    return lax.dot_general(left, right, (dims, ((), ())), preferred_element_type=F32)


def fused_kernel(
    groups, columns, global_ref, q_ref, k_ref, v_ref, g_ref,
    att_ref, dq_ref, dk_ref, dv_ref,
    qg, kv, side, cand, piece, glob, dsum, dside, dside_in, dg_out, dg_in, dg_sum,
    att_out, dq_out, dk_out, dv_out,
    local_sem, in_send, in_recv, side_send, side_recv, ga_send, ga_recv, gb_send, gb_recv,
    ds_send, ds_recv, da_send, da_recv, db_send, db_recv, out_send, out_recv,
):
    h = lax.axis_index("grp")
    c = lax.axis_index("seq")
    rows, width = q_ref.shape
    share = width // groups
    strip = rows // columns
    pairs = share // LANES

    def rows_of(index):
        return pl.ds(pl.multiple_of(index * strip, strip), strip)

    def remote(src, dst, send, recv, device):
        return pltpu.make_async_remote_copy(
            src_ref=src, dst_ref=dst, send_sem=send, recv_sem=recv,
            device_id=device, device_id_type=MESH,
        )

    right = lax.rem(c + 1, columns)
    left = lax.rem(c + columns - 1, columns)

    barrier = pltpu.get_barrier_semaphore()
    for d in range(1, groups):
        pl.semaphore_signal(
            barrier, inc=1, device_id=(lax.rem(h + d, groups), c), device_id_type=MESH
        )
    for e in range(1, columns):
        pl.semaphore_signal(
            barrier, inc=1, device_id=(h, lax.rem(c + e, columns)), device_id_type=MESH
        )

    def lanes_of(index, pair):
        return pl.ds(pl.multiple_of(index * share + pair * LANES, LANES), LANES)

    sources = []
    for pair in range(pairs):
        where = functools.partial(lanes_of, pair=pair)
        for a, ref in enumerate((k_ref, v_ref)):
            sources.append((ref, where, kv.at[pair, a]))
        for a, ref in enumerate((q_ref, g_ref)):
            sources.append((ref, where, qg.at[pair, a]))
    own = [
        pltpu.make_async_copy(ref.at[:, where(h)], buf.at[h], local_sem.at[n])
        for n, (ref, where, buf) in enumerate(sources)
    ]
    for copy in own:
        copy.start()
    pl.semaphore_wait(barrier, groups + columns - 2)

    incoming = {}

    def send_in(*numbers):
        for d in range(1, groups):
            target = lax.rem(h + d, groups)
            for n in numbers:
                ref, where, buf = sources[n]
                incoming[n, d] = remote(
                    ref.at[:, where(target)], buf.at[h],
                    in_send.at[n, d - 1], in_recv.at[n, d - 1], (target, c),
                )
                incoming[n, d].start()

    def side_copies(pair, d):
        segment = lax.rem(h + groups - d, groups)
        return [
            remote(
                kv.at[pair, :, segment], side.at[pair, way, :, segment],
                side_send.at[way, pair, d], side_recv.at[way, pair, d], (h, to),
            )
            for way, to in ((0, right), (1, left))
        ]

    def forward(pair, then):
        own[4 * pair].wait()
        own[4 * pair + 1].wait()
        for copy in side_copies(pair, 0):
            copy.start()
        for d in range(1, groups):
            incoming[4 * pair, d].wait_recv()
            incoming[4 * pair + 1, d].wait_recv()
            for copy in side_copies(pair, d):
                copy.start()
            if d == 1:
                send_in(*then)

    seg_of = [lax.div(global_ref[w], columns) for w in range(GLOBALS)]
    col_of = [lax.rem(global_ref[w], columns) for w in range(GLOBALS)]

    def offer(pair):
        for w in range(GLOBALS):
            for a in range(2):
                chosen = kv[pair, a, 0]
                for t in range(1, groups):
                    chosen = jnp.where(seg_of[w] == t, kv[pair, a, t], chosen)
                cand[pair, 2 * w + a] = chosen
        copies = []
        for e in range(1, columns):
            to = lax.rem(c + e, columns)
            copies.append(
                remote(
                    cand.at[pair, :, rows_of(to), :], piece.at[pair, c],
                    ga_send.at[pair, e - 1], ga_recv.at[pair, e - 1], (h, to),
                )
            )
            copies[-1].start()
        piece[pair, c] = cand[pair, :, rows_of(c), :]
        return copies

    def choose(pair, before):
        for copy in before:
            copy.wait_recv()
        for w in range(GLOBALS):
            for a in range(2):
                chosen = piece[pair, 0, 2 * w + a]
                for e in range(1, columns):
                    chosen = jnp.where(col_of[w] == e, piece[pair, e, 2 * w + a], chosen)
                glob[pair, 2 * w + a, rows_of(c), :] = chosen
        copies = []
        for e in range(1, columns):
            to = lax.rem(c + e, columns)
            copies.append(
                remote(
                    glob.at[pair, :, rows_of(c), :], glob.at[pair, :, rows_of(c), :],
                    gb_send.at[pair, e - 1], gb_recv.at[pair, e - 1], (h, to),
                )
            )
            copies[-1].start()
        return copies

    lane = lax.broadcasted_iota(jnp.int32, (rows, LANES), 1)
    factor = 1.0 / math.sqrt(HEAD_DIM)
    last = groups * columns - 1

    def stacked(block):
        zero = jnp.zeros_like(block)
        low = jnp.where(lane < HEAD_DIM, block, zero)
        high = jnp.where(lane < HEAD_DIM, zero, block)
        return jnp.concatenate([low, high], axis=0)

    def picked(wide):
        return jnp.concatenate(
            [wide[:HEAD_DIM, :rows], wide[HEAD_DIM:, rows:]], axis=0
        ).T

    outgoing = ((att_out, att_ref), (dq_out, dq_ref), (dk_out, dk_ref), (dv_out, dv_ref))

    def out_copies(pair, i, start, stop):
        segment = lax.rem(h + i + 1, groups)
        return [
            remote(
                buf.at[pair, segment], ref.at[:, lanes_of(h, pair)],
                out_send.at[n, pair, i], out_recv.at[n, pair, i], (segment, c),
            )
            for n, (buf, ref) in tuple(enumerate(outgoing))[start:stop]
        ]

    def dside_copies(pair, j):
        steps = pl.ds(2 * j, 2)
        return [
            remote(
                dside.at[pair, way, :, steps], dside_in.at[pair, way, :, steps],
                ds_send.at[way, pair, j], ds_recv.at[way, pair, j], (h, to),
            )
            for way, to in ((0, left), (1, right))
        ]

    at_first = jnp.where(c == 0, 1, 0)
    at_last = jnp.where(c == columns - 1, 1, 0)
    dense = (groups + GLOBALS) * rows

    def unit(pair, i):
        segment = lax.rem(h + i + 1, groups)
        block = segment * columns + c
        before = lax.rem(segment + groups - at_first, groups)
        after = lax.rem(segment + at_last, groups)

        def listed(a):
            return jnp.concatenate(
                [kv[pair, a, t] for t in range(groups)]
                + [glob[pair, 2 * w + a] for w in range(GLOBALS)]
                + [side[pair, 0, a, before], side[pair, 1, a, after]],
                axis=0,
            )

        key = listed(0)
        value = listed(1)
        query = stacked(qg[pair, 0, segment] * jnp.asarray(factor, BF16))
        grad = stacked(qg[pair, 1, segment])
        scores = contract(key, query, ((1,), (1,)))
        scores = jnp.concatenate(
            [
                scores[:dense],
                jnp.where(block > 0, scores[dense : dense + rows], -1e30),
                jnp.where(block < last, scores[dense + rows :], -1e30),
            ],
            axis=0,
        )
        raised = jnp.exp(scores - jnp.max(scores, axis=0, keepdims=True))
        prob = raised * (1.0 / jnp.sum(raised, axis=0, keepdims=True))
        half = prob.astype(BF16)
        d_prob = contract(value, grad, ((1,), (1,)))
        result = contract(value, half, ((0,), (0,)))
        row_dot = jnp.sum(prob * d_prob, axis=0, keepdims=True)
        d_scores = (prob * (d_prob - row_dot)).astype(BF16)
        d_query = contract(key, d_scores, ((0,), (0,))) * factor
        d_value = contract(half, grad, ((1,), (0,)))
        d_key = contract(d_scores, query, ((1,), (0,)))
        att_out[pair, segment] = picked(result).astype(BF16)
        dq_out[pair, segment] = picked(d_query).astype(BF16)
        return d_key, d_value

    def halves(pair, j):
        both = [unit(pair, i) for i in (2 * j, 2 * j + 1)]
        for a in range(2):
            summed = both[0][a][:dense] + both[1][a][:dense]
            if j == 0:
                dsum[pair, a] = summed
            else:
                dsum[pair, a] += summed
            for i in range(2):
                dside[pair, 0, a, 2 * j + i] = both[i][a][dense : dense + rows].astype(BF16)
                dside[pair, 1, a, 2 * j + i] = both[i][a][dense + rows :].astype(BF16)
        for copy in dside_copies(pair, j):
            copy.start()
        for i in (2 * j, 2 * j + 1):
            if i < groups - 1:
                for copy in out_copies(pair, i, 0, 2):
                    copy.start()
            else:
                att_ref[:, lanes_of(h, pair)] = att_out[pair, h]
                dq_ref[:, lanes_of(h, pair)] = dq_out[pair, h]

    def arrive(pair, before):
        for n in (4 * pair + 2, 4 * pair + 3):
            own[n].wait()
            for d in range(1, groups):
                incoming[n, d].wait_recv()
        for d in range(groups):
            for copy in side_copies(pair, d):
                copy.wait_recv()
        for copy in before:
            copy.wait_recv()

    def scatter(pair):
        for w in range(GLOBALS):
            for a in range(2):
                start = (groups + w) * rows
                dg_out[pair, 2 * w + a] = dsum[pair, a, start : start + rows].astype(BF16)
        copies = []
        for e in range(1, columns):
            to = lax.rem(c + e, columns)
            copies.append(
                remote(
                    dg_out.at[pair, :, rows_of(to), :], dg_in.at[pair, c],
                    da_send.at[pair, e - 1], da_recv.at[pair, e - 1], (h, to),
                )
            )
            copies[-1].start()
        dg_in[pair, c] = dg_out[pair, :, rows_of(c), :]
        return copies

    def gather(pair, before):
        for copy in before:
            copy.wait_recv()
        total = dg_in[pair, 0].astype(F32)
        for e in range(1, columns):
            total = total + dg_in[pair, e].astype(F32)
        dg_sum[pair, :, rows_of(c), :] = total.astype(BF16)
        copies = []
        for e in range(1, columns):
            to = lax.rem(c + e, columns)
            copies.append(
                remote(
                    dg_sum.at[pair, :, rows_of(c), :], dg_sum.at[pair, :, rows_of(c), :],
                    db_send.at[pair, e - 1], db_recv.at[pair, e - 1], (h, to),
                )
            )
            copies[-1].start()
        return copies

    def finish(pair, before):
        for j in range(groups // 2):
            for copy in dside_copies(pair, j):
                copy.wait_recv()
        for copy in before:
            copy.wait_recv()
        for i in range(groups):
            segment = lax.rem(h + i + 1, groups)
            low = lax.rem(i + at_last, groups)
            high = lax.rem(i + groups - at_first, groups)
            span = pl.ds(pl.multiple_of(segment * rows, rows), rows)
            for a, buf in enumerate((dk_out, dv_out)):
                whole = dsum[pair, a, span]
                whole += dside_in[pair, 0, a, low].astype(F32)
                whole += dside_in[pair, 1, a, high].astype(F32)
                for w in range(GLOBALS):
                    mine = (global_ref[w] == segment * columns + c).astype(F32)
                    whole += dg_sum[pair, 2 * w + a].astype(F32) * mine
                buf[pair, segment] = whole.astype(BF16)
            if i < groups - 1:
                for copy in out_copies(pair, i, 2, 4):
                    copy.start()
        dk_ref[:, lanes_of(h, pair)] = dk_out[pair, h]
        dv_ref[:, lanes_of(h, pair)] = dv_out[pair, h]

    firsts, seconds, thirds, fourths = [], [], [], []

    def prepare(pair):
        more = range(4 * pair + 4, min(4 * pair + 6, 4 * pairs))
        forward(pair, (4 * pair + 2, 4 * pair + 3))
        firsts.append(offer(pair))
        send_in(*more)

    send_in(0, 1)
    prepare(0)
    seconds.append(choose(0, firsts[0]))
    for pair in range(pairs):
        if pair + 1 < pairs:
            prepare(pair + 1)
        arrive(pair, seconds[pair])
        halves(pair, 0)
        if pair + 1 < pairs:
            seconds.append(choose(pair + 1, firsts[pair + 1]))
        if pair:
            fourths.append(gather(pair - 1, thirds[-1]))
        halves(pair, 1)
        thirds.append(scatter(pair))
        if pair:
            finish(pair - 1, fourths[-1])
    fourths.append(gather(pairs - 1, thirds[-1]))
    finish(pairs - 1, fourths[-1])

    for copy in incoming.values():
        copy.wait_send()
    for copy in sum(firsts + seconds + thirds + fourths, []):
        copy.wait_send()
    for pair in range(pairs):
        for d in range(groups):
            for copy in side_copies(pair, d):
                copy.wait_send()
        for j in range(groups // 2):
            for copy in dside_copies(pair, j):
                copy.wait_send()
        for i in range(groups - 1):
            for copy in out_copies(pair, i, 0, 4):
                copy.wait()


def fused(groups, columns, query, keys, values, d_out, rand_blocks, global_blocks):
    rows, width = query.shape
    share = width // groups
    strip = rows // columns
    half = functools.partial(pltpu.VMEM, dtype=BF16)
    full = functools.partial(pltpu.VMEM, dtype=F32)
    dma = pltpu.SemaphoreType.DMA
    peers = (columns - 1,)
    pairs = share // LANES
    tile = (rows, LANES)
    scratch = [
        half((pairs, 2, groups, *tile)),
        half((pairs, 2, groups, *tile)),
        half((pairs, 2, 2, groups, *tile)),
        half((pairs, 2 * GLOBALS, *tile)),
        half((pairs, columns, 2 * GLOBALS, strip, LANES)),
        half((pairs, 2 * GLOBALS, *tile)),
        full((pairs, 2, (groups + GLOBALS) * rows, LANES)),
        half((pairs, 2, 2, groups, *tile)),
        half((pairs, 2, 2, groups, *tile)),
        half((pairs, 2 * GLOBALS, *tile)),
        half((pairs, columns, 2 * GLOBALS, strip, LANES)),
        half((pairs, 2 * GLOBALS, *tile)),
    ] + [half((pairs, groups, *tile))] * 4
    arrays = 4 * pairs
    steps = (2, pairs, groups // 2)
    scratch += [dma((arrays,))]
    scratch += [dma((arrays, groups - 1))] * 2 + [dma((2, pairs, groups))] * 2
    scratch += [dma((pairs, *peers))] * 4
    scratch += [dma(steps)] * 2 + [dma((pairs, *peers))] * 4
    scratch += [dma((4, pairs, groups - 1))] * 2
    vmem = pl.BlockSpec(memory_space=pltpu.VMEM)
    hbm = pl.BlockSpec(memory_space=pltpu.HBM)
    return pl.pallas_call(
        functools.partial(fused_kernel, groups, columns),
        out_shape=[jax.ShapeDtypeStruct((rows, width), BF16)] * 4,
        in_specs=[pl.BlockSpec(memory_space=pltpu.SMEM)] + [hbm] * 4,
        out_specs=[vmem] * 4,
        scratch_shapes=scratch,
        compiler_params=pltpu.CompilerParams(
            collective_id=0, has_side_effects=True, vmem_limit_bytes=63 * 2**20
        ),
    )(global_blocks, query, keys, values, d_out)


def solution(mesh):
    in_specs = (
        P(("grp", "seq"), None),
        P(("grp", "seq"), None),
        P(("grp", "seq"), None),
        P(("grp", "seq"), None),
        P(),
        P(),
    )
    out_specs = (
        P(("grp", "seq"), None),
        P(("grp", "seq"), None),
        P(("grp", "seq"), None),
        P(("grp", "seq"), None),
    )
    groups, columns = mesh.shape["grp"], mesh.shape["seq"]

    def run(query, *rest):
        rows, width = query.shape
        whole_column = rows == BLOCK and groups - 1 == RANDOMS and groups % 2 == 0
        if whole_column and rows % (16 * columns) == 0 and width % (groups * LANES) == 0:
            return fused(groups, columns, query, *rest)
        return body(query, *rest)

    return jax.shard_map(run, mesh=mesh, in_specs=in_specs, out_specs=out_specs, check_vma=False)
```

profile of v0, /device:TPU:0, one launch (start us, length us, event | category | flops | bytes accessed | tf_op | source)
XLA Modules:
  0.0 70.1 jit_solution(17241990701130270737)
XLA Ops:
  0.6 64.9 %shard_map.84 = (bf16[128,1024]{1,0:T(8,128)(2,1)}, bf16[128,1024]{1,0:T(8,128)(2,1)}, bf16[128,1024]{1,0:T(8,128)(2,1)}, bf16[128,1024]{1,0:T(8,128)(2,1)}) custom-call(s32[2]{0:T(128)} %global_ref.1, bf16[128,1024]{1,0:T(8,128)(2,1)} %q_ref.1, bf16[128,1024]{1,0:T(8,128)(2,1)} %k_ref.1, bf16[128,1024]{1,0:T(8,128)(2,1)} %v_ref.1, bf16[128,1024]{1,0:T(8,128)(2,1)} %g_ref.1), custom_call_target="tpu_custom_call" | custom-call | tf_op jit(solution)/shard_map/pallas_call | solution.py:603
  65.6 0.0 copy-start.2
  65.6 1.7 %copy.13 = bf16[128,1024]{1,0:T(8,128)(2,1)} copy(bf16[128,1024]{1,0:T(8,128)(2,1)} %get-tuple-element.8) | data formatting | bytes 524288
  67.3 0.0 copy-done.2
  67.3 0.0 copy-start.1
  67.3 0.7 %copy.14 = bf16[128,1024]{1,0:T(8,128)(2,1)} copy(bf16[128,1024]{1,0:T(8,128)(2,1)S(1)} %copy-done.2) | data formatting | bytes 524288
  68.0 0.3 copy-done.1
  68.3 0.0 copy-start
  68.3 0.7 %copy.15 = bf16[128,1024]{1,0:T(8,128)(2,1)} copy(bf16[128,1024]{1,0:T(8,128)(2,1)S(1)} %copy-done.1) | data formatting | bytes 524288
  69.1 0.3 copy-done
  69.4 0.7 %copy.16 = bf16[128,1024]{1,0:T(8,128)(2,1)} copy(bf16[128,1024]{1,0:T(8,128)(2,1)S(1)} %copy-done) | data formatting | bytes 524288
Async XLA Ops:
  65.6 1.7 %copy-start.2 = (bf16[128,1024]{1,0:T(8,128)(2,1)S(1)}, bf16[128,1024]{1,0:T(8,128)(2,1)}, u32[]{:S(2)}) copy-start(bf16[128,1024]{1,0:T(8,128)(2,1)} %get-tuple-element.9) | copy-start | bytes 786436
  67.3 1.0 %copy-start.1 = (bf16[128,1024]{1,0:T(8,128)(2,1)S(1)}, bf16[128,1024]{1,0:T(8,128)(2,1)}, u32[]{:S(2)}) copy-start(bf16[128,1024]{1,0:T(8,128)(2,1)} %get-tuple-element.10) | copy-start | bytes 786436
  68.3 1.0 %copy-start = (bf16[128,1024]{1,0:T(8,128)(2,1)S(1)}, bf16[128,1024]{1,0:T(8,128)(2,1)}, u32[]{:S(2)}) copy-start(bf16[128,1024]{1,0:T(8,128)(2,1)} %get-tuple-element.11) | copy-start | bytes 786436
where the time goes:
time: 70.3 us; the launch traced here: 70.1 us
  Pallas kernels  64.9 us (92%)
  local copies, waits for them, and re-layouts  4.5 us (6%)
    pallas_call x1, Pallas kernels, fused(): pl.pallas_call(functools.partial(fused_kernel, groups, columns), out_shap...  64.9 us
    unnamed x10, local copies, waits for them, and re-layouts  4.5 us

commit v1 on v0

--- a/solution.py
+++ b/solution.py
@@ -218,8 +218,8 @@
     att_ref, dq_ref, dk_ref, dv_ref,
     qg, kv, side, cand, piece, glob, dsum, dside, dside_in, dg_out, dg_in, dg_sum,
     att_out, dq_out, dk_out, dv_out,
-    local_sem, in_send, in_recv, side_send, side_recv, ga_send, ga_recv, gb_send, gb_recv,
-    ds_send, ds_recv, da_send, da_recv, db_send, db_recv, out_send, out_recv,
+    own_sem, kv_recv, qg_recv, side_recv, ga_recv, gb_recv, ds_recv, da_recv, db_recv,
+    in_send, side_send, glob_send, ds_send, out_send, out_recv, keep_sem,
 ):
     h = lax.axis_index("grp")
     c = lax.axis_index("seq")
@@ -236,6 +236,9 @@
             src_ref=src, dst_ref=dst, send_sem=send, recv_sem=recv,
             device_id=device, device_id_type=MESH,
         )
+
+    def settle(ref, sem):
+        pltpu.make_async_copy(ref, ref, sem).wait()
 
     right = lax.rem(c + 1, columns)
     left = lax.rem(c + columns - 1, columns)
@@ -253,55 +256,45 @@
     def lanes_of(index, pair):
         return pl.ds(pl.multiple_of(index * share + pair * LANES, LANES), LANES)
 
-    sources = []
+    own = []
     for pair in range(pairs):
-        where = functools.partial(lanes_of, pair=pair)
-        for a, ref in enumerate((k_ref, v_ref)):
-            sources.append((ref, where, kv.at[pair, a]))
-        for a, ref in enumerate((q_ref, g_ref)):
-            sources.append((ref, where, qg.at[pair, a]))
-    own = [
-        pltpu.make_async_copy(ref.at[:, where(h)], buf.at[h], local_sem.at[n])
-        for n, (ref, where, buf) in enumerate(sources)
-    ]
+        for kind, (refs, buf) in enumerate((((k_ref, v_ref), kv), ((q_ref, g_ref), qg))):
+            for a, ref in enumerate(refs):
+                own.append(
+                    pltpu.make_async_copy(
+                        ref.at[:, lanes_of(h, pair)], buf.at[pair, a, h], own_sem.at[kind, pair]
+                    )
+                )
     for copy in own:
         copy.start()
     pl.semaphore_wait(barrier, groups + columns - 2)
 
-    incoming = {}
-
-    def send_in(*numbers):
+    def send_in(kind, pair):
+        refs, buf = (((k_ref, v_ref), kv), ((q_ref, g_ref), qg))[kind]
         for d in range(1, groups):
             target = lax.rem(h + d, groups)
-            for n in numbers:
-                ref, where, buf = sources[n]
-                incoming[n, d] = remote(
-                    ref.at[:, where(target)], buf.at[h],
-                    in_send.at[n, d - 1], in_recv.at[n, d - 1], (target, c),
-                )
-                incoming[n, d].start()
-
-    def side_copies(pair, d):
+            arrival = qg_recv.at[pair] if kind else kv_recv.at[pair, d - 1]
+            for a, ref in enumerate(refs):
+                remote(
+                    ref.at[:, lanes_of(target, pair)], buf.at[pair, a, h],
+                    in_send.at[kind], arrival, (target, c),
+                ).start()
+
+    def send_sides(pair, d):
         segment = lax.rem(h + groups - d, groups)
-        return [
+        for way, to in ((0, right), (1, left)):
             remote(
                 kv.at[pair, :, segment], side.at[pair, way, :, segment],
-                side_send.at[way, pair, d], side_recv.at[way, pair, d], (h, to),
-            )
-            for way, to in ((0, right), (1, left))
-        ]
-
-    def forward(pair, then):
-        own[4 * pair].wait()
-        own[4 * pair + 1].wait()
-        for copy in side_copies(pair, 0):
-            copy.start()
+                side_send.at[0], side_recv.at[pair], (h, to),
+            ).start()
+
+    def forward(pair, then=None):
+        settle(kv.at[pair, :, h], own_sem.at[0, pair])
+        send_sides(pair, 0)
         for d in range(1, groups):
-            incoming[4 * pair, d].wait_recv()
-            incoming[4 * pair + 1, d].wait_recv()
-            for copy in side_copies(pair, d):
-                copy.start()
-            if d == 1:
+            settle(kv.at[pair, :, lax.rem(h + groups - d, groups)], kv_recv.at[pair, d - 1])
+            send_sides(pair, d)
+            if d == 1 and then is not None:
                 send_in(*then)
 
     seg_of = [lax.div(global_ref[w], columns) for w in range(GLOBALS)]
@@ -314,39 +307,28 @@
                 for t in range(1, groups):
                     chosen = jnp.where(seg_of[w] == t, kv[pair, a, t], chosen)
                 cand[pair, 2 * w + a] = chosen
-        copies = []
         for e in range(1, columns):
             to = lax.rem(c + e, columns)
-            copies.append(
-                remote(
-                    cand.at[pair, :, rows_of(to), :], piece.at[pair, c],
-                    ga_send.at[pair, e - 1], ga_recv.at[pair, e - 1], (h, to),
-                )
-            )
-            copies[-1].start()
+            remote(
+                cand.at[pair, :, rows_of(to), :], piece.at[pair, c],
+                glob_send.at[0], ga_recv.at[pair], (h, to),
+            ).start()
         piece[pair, c] = cand[pair, :, rows_of(c), :]
-        return copies
-
-    def choose(pair, before):
-        for copy in before:
-            copy.wait_recv()
+
+    def choose(pair):
+        settle(piece.at[pair, pl.ds(0, columns - 1)], ga_recv.at[pair])
         for w in range(GLOBALS):
             for a in range(2):
                 chosen = piece[pair, 0, 2 * w + a]
                 for e in range(1, columns):
                     chosen = jnp.where(col_of[w] == e, piece[pair, e, 2 * w + a], chosen)
                 glob[pair, 2 * w + a, rows_of(c), :] = chosen
-        copies = []
         for e in range(1, columns):
             to = lax.rem(c + e, columns)
-            copies.append(
-                remote(
-                    glob.at[pair, :, rows_of(c), :], glob.at[pair, :, rows_of(c), :],
-                    gb_send.at[pair, e - 1], gb_recv.at[pair, e - 1], (h, to),
-                )
-            )
-            copies[-1].start()
-        return copies
+            remote(
+                glob.at[pair, :, rows_of(c), :], glob.at[pair, :, rows_of(c), :],
+                glob_send.at[1], gb_recv.at[pair], (h, to),
+            ).start()
 
     lane = lax.broadcasted_iota(jnp.int32, (rows, LANES), 1)
     factor = 1.0 / math.sqrt(HEAD_DIM)
@@ -365,25 +347,26 @@
 
     outgoing = ((att_out, att_ref), (dq_out, dq_ref), (dk_out, dk_ref), (dv_out, dv_ref))
 
-    def out_copies(pair, i, start, stop):
+    def send_out(pair, i, first):
         segment = lax.rem(h + i + 1, groups)
-        return [
-            remote(
-                buf.at[pair, segment], ref.at[:, lanes_of(h, pair)],
-                out_send.at[n, pair, i], out_recv.at[n, pair, i], (segment, c),
-            )
-            for n, (buf, ref) in tuple(enumerate(outgoing))[start:stop]
-        ]
-
-    def dside_copies(pair, j):
+        for buf, ref in outgoing[first : first + 2]:
+            if i < groups - 1:
+                remote(
+                    buf.at[pair, segment], ref.at[:, lanes_of(h, pair)],
+                    out_send.at[first // 2], out_recv.at[first // 2], (segment, c),
+                ).start()
+            else:
+                pltpu.make_async_copy(
+                    buf.at[pair, h], ref.at[:, lanes_of(h, pair)], keep_sem.at[0]
+                ).start()
+
+    def send_dsides(pair, j):
         steps = pl.ds(2 * j, 2)
-        return [
+        for way, to in ((0, left), (1, right)):
             remote(
                 dside.at[pair, way, :, steps], dside_in.at[pair, way, :, steps],
-                ds_send.at[way, pair, j], ds_recv.at[way, pair, j], (h, to),
-            )
-            for way, to in ((0, left), (1, right))
-        ]
+                ds_send.at[0], ds_recv.at[pair], (h, to),
+            ).start()
 
     at_first = jnp.where(c == 0, 1, 0)
     at_last = jnp.where(c == columns - 1, 1, 0)
@@ -441,70 +424,45 @@
             for i in range(2):
                 dside[pair, 0, a, 2 * j + i] = both[i][a][dense : dense + rows].astype(BF16)
                 dside[pair, 1, a, 2 * j + i] = both[i][a][dense + rows :].astype(BF16)
-        for copy in dside_copies(pair, j):
-            copy.start()
+        send_dsides(pair, j)
         for i in (2 * j, 2 * j + 1):
-            if i < groups - 1:
-                for copy in out_copies(pair, i, 0, 2):
-                    copy.start()
-            else:
-                att_ref[:, lanes_of(h, pair)] = att_out[pair, h]
-                dq_ref[:, lanes_of(h, pair)] = dq_out[pair, h]
-
-    def arrive(pair, before):
-        for n in (4 * pair + 2, 4 * pair + 3):
-            own[n].wait()
-            for d in range(1, groups):
-                incoming[n, d].wait_recv()
-        for d in range(groups):
-            for copy in side_copies(pair, d):
-                copy.wait_recv()
-        for copy in before:
-            copy.wait_recv()
+            send_out(pair, i, 0)
+
+    def arrive(pair):
+        settle(qg.at[pair, :, h], own_sem.at[1, pair])
+        settle(qg.at[pair, :, pl.ds(0, groups - 1)], qg_recv.at[pair])
+        settle(side.at[pair], side_recv.at[pair])
+        settle(glob.at[pair, :, pl.ds(0, rows - strip)], gb_recv.at[pair])
 
     def scatter(pair):
         for w in range(GLOBALS):
             for a in range(2):
                 start = (groups + w) * rows
                 dg_out[pair, 2 * w + a] = dsum[pair, a, start : start + rows].astype(BF16)
-        copies = []
         for e in range(1, columns):
             to = lax.rem(c + e, columns)
-            copies.append(
-                remote(
-                    dg_out.at[pair, :, rows_of(to), :], dg_in.at[pair, c],
-                    da_send.at[pair, e - 1], da_recv.at[pair, e - 1], (h, to),
-                )
-            )
-            copies[-1].start()
+            remote(
+                dg_out.at[pair, :, rows_of(to), :], dg_in.at[pair, c],
+                glob_send.at[2], da_recv.at[pair], (h, to),
+            ).start()
         dg_in[pair, c] = dg_out[pair, :, rows_of(c), :]
-        return copies
-
-    def gather(pair, before):
-        for copy in before:
-            copy.wait_recv()
+
+    def gather(pair):
+        settle(dg_in.at[pair, pl.ds(0, columns - 1)], da_recv.at[pair])
         total = dg_in[pair, 0].astype(F32)
         for e in range(1, columns):
             total = total + dg_in[pair, e].astype(F32)
         dg_sum[pair, :, rows_of(c), :] = total.astype(BF16)
-        copies = []
         for e in range(1, columns):
             to = lax.rem(c + e, columns)
-            copies.append(
-                remote(
-                    dg_sum.at[pair, :, rows_of(c), :], dg_sum.at[pair, :, rows_of(c), :],
-                    db_send.at[pair, e - 1], db_recv.at[pair, e - 1], (h, to),
-                )
-            )
-            copies[-1].start()
-        return copies
-
-    def finish(pair, before):
-        for j in range(groups // 2):
-            for copy in dside_copies(pair, j):
-                copy.wait_recv()
-        for copy in before:
-            copy.wait_recv()
+            remote(
+                dg_sum.at[pair, :, rows_of(c), :], dg_sum.at[pair, :, rows_of(c), :],
+                glob_send.at[3], db_recv.at[pair], (h, to),
+            ).start()
+
+    def finish(pair):
+        settle(dside_in.at[pair], ds_recv.at[pair])
+        settle(dg_sum.at[pair, :, pl.ds(0, rows - strip)], db_recv.at[pair])
         for i in range(groups):
             segment = lax.rem(h + i + 1, groups)
             low = lax.rem(i + at_last, groups)
@@ -518,53 +476,39 @@
                     mine = (global_ref[w] == segment * columns + c).astype(F32)
                     whole += dg_sum[pair, 2 * w + a].astype(F32) * mine
                 buf[pair, segment] = whole.astype(BF16)
-            if i < groups - 1:
-                for copy in out_copies(pair, i, 2, 4):
-                    copy.start()
-        dk_ref[:, lanes_of(h, pair)] = dk_out[pair, h]
-        dv_ref[:, lanes_of(h, pair)] = dv_out[pair, h]
-
-    firsts, seconds, thirds, fourths = [], [], [], []
-
-    def prepare(pair):
-        more = range(4 * pair + 4, min(4 * pair + 6, 4 * pairs))
-        forward(pair, (4 * pair + 2, 4 * pair + 3))
-        firsts.append(offer(pair))
-        send_in(*more)
-
-    send_in(0, 1)
-    prepare(0)
-    seconds.append(choose(0, firsts[0]))
+            send_out(pair, i, 2)
+
+    send_in(0, 0)
     for pair in range(pairs):
         if pair + 1 < pairs:
-            prepare(pair + 1)
-        arrive(pair, seconds[pair])
+            send_in(0, pair + 1)
+        forward(pair, (1, pair))
+        offer(pair)
+    for pair in range(pairs):
+        choose(pair)
+    for pair in range(pairs):
+        arrive(pair)
         halves(pair, 0)
-        if pair + 1 < pairs:
-            seconds.append(choose(pair + 1, firsts[pair + 1]))
         if pair:
-            fourths.append(gather(pair - 1, thirds[-1]))
+            gather(pair - 1)
         halves(pair, 1)
-        thirds.append(scatter(pair))
+        scatter(pair)
         if pair:
-            finish(pair - 1, fourths[-1])
-    fourths.append(gather(pairs - 1, thirds[-1]))
-    finish(pairs - 1, fourths[-1])
-
-    for copy in incoming.values():
-        copy.wait_send()
-    for copy in sum(firsts + seconds + thirds + fourths, []):
-        copy.wait_send()
-    for pair in range(pairs):
-        for d in range(groups):
-            for copy in side_copies(pair, d):
-                copy.wait_send()
-        for j in range(groups // 2):
-            for copy in dside_copies(pair, j):
-                copy.wait_send()
-        for i in range(groups - 1):
-            for copy in out_copies(pair, i, 0, 4):
-                copy.wait()
+            finish(pair - 1)
+    gather(pairs - 1)
+    finish(pairs - 1)
+
+    shares = pl.ds(0, groups - 1)
+    for n in range(2):
+        settle(kv.at[:, :, shares], in_send.at[n])
+        settle(kv.at[:, :, shares], out_send.at[n])
+        settle(kv.at[:, :, shares], out_recv.at[n])
+    settle(side, side_send.at[0])
+    settle(dside, ds_send.at[0])
+    for n in range(2):
+        settle(piece.at[:, pl.ds(0, columns - 1)], glob_send.at[2 * n])
+        settle(glob.at[:, :, pl.ds(0, rows - strip)], glob_send.at[2 * n + 1])
+    settle(kv.at[:, :, pl.ds(0, 2)], keep_sem.at[0])
 
 
 def fused(groups, columns, query, keys, values, d_out, rand_blocks, global_blocks):
@@ -574,7 +518,6 @@
     half = functools.partial(pltpu.VMEM, dtype=BF16)
     full = functools.partial(pltpu.VMEM, dtype=F32)
     dma = pltpu.SemaphoreType.DMA
-    peers = (columns - 1,)
     pairs = share // LANES
     tile = (rows, LANES)
     scratch = [
@@ -591,20 +534,14 @@
         half((pairs, columns, 2 * GLOBALS, strip, LANES)),
         half((pairs, 2 * GLOBALS, *tile)),
     ] + [half((pairs, groups, *tile))] * 4
-    arrays = 4 * pairs
-    steps = (2, pairs, groups // 2)
-    scratch += [dma((arrays,))]
-    scratch += [dma((arrays, groups - 1))] * 2 + [dma((2, pairs, groups))] * 2
-    scratch += [dma((pairs, *peers))] * 4
-    scratch += [dma(steps)] * 2 + [dma((pairs, *peers))] * 4
-    scratch += [dma((4, pairs, groups - 1))] * 2
-    vmem = pl.BlockSpec(memory_space=pltpu.VMEM)
+    scratch += [dma((2, pairs)), dma((pairs, groups - 1))] + [dma((pairs,))] * 7
+    scratch += [dma((2,)), dma((1,)), dma((4,)), dma((1,)), dma((2,)), dma((2,)), dma((1,))]
     hbm = pl.BlockSpec(memory_space=pltpu.HBM)
     return pl.pallas_call(
         functools.partial(fused_kernel, groups, columns),
         out_shape=[jax.ShapeDtypeStruct((rows, width), BF16)] * 4,
         in_specs=[pl.BlockSpec(memory_space=pltpu.SMEM)] + [hbm] * 4,
-        out_specs=[vmem] * 4,
+        out_specs=[hbm] * 4,
         scratch_shapes=scratch,
         compiler_params=pltpu.CompilerParams(
             collective_id=0, has_side_effects=True, vmem_limit_bytes=63 * 2**20
@@ -612,6 +549,42 @@
     )(global_blocks, query, keys, values, d_out)
 
 
+CHUNKS = 4
+
+
+def relay_kernel(*refs):
+    count = (len(refs) - 3) // 2
+    sources, targets = refs[:count], refs[count : 2 * count]
+    held, in_sem, out_sem = refs[2 * count :]
+    rows = held.shape[1] // CHUNKS
+    for part in range(CHUNKS):
+        at = pl.ds(part * rows, rows)
+        for n in range(count):
+            pltpu.make_async_copy(sources[n].at[at], held.at[n, at], in_sem.at[part]).start()
+    for part in range(CHUNKS):
+        at = pl.ds(part * rows, rows)
+        pltpu.make_async_copy(held.at[:, at], held.at[:, at], in_sem.at[part]).wait()
+        for n in range(count):
+            pltpu.make_async_copy(held.at[n, at], targets[n].at[at], out_sem.at[0]).start()
+    pltpu.make_async_copy(held, held, out_sem.at[0]).wait()
+
+
+def relay(*arrays):
+    hbm = pl.BlockSpec(memory_space=pltpu.HBM)
+    count = len(arrays)
+    return pl.pallas_call(
+        relay_kernel,
+        out_shape=[jax.ShapeDtypeStruct(a.shape, a.dtype) for a in arrays],
+        in_specs=[hbm] * count,
+        out_specs=[hbm] * count,
+        scratch_shapes=[
+            pltpu.VMEM((count, *arrays[0].shape), arrays[0].dtype),
+            pltpu.SemaphoreType.DMA((CHUNKS,)),
+            pltpu.SemaphoreType.DMA((1,)),
+        ],
+    )(*arrays)
+
+
 def solution(mesh):
     in_specs = (
         P(("grp", "seq"), None),
@@ -633,7 +606,7 @@
         rows, width = query.shape
         whole_column = rows == BLOCK and groups - 1 == RANDOMS and groups % 2 == 0
         if whole_column and rows % (16 * columns) == 0 and width % (groups * LANES) == 0:
-            return fused(groups, columns, query, *rest)
+            return relay(*fused(groups, columns, query, *rest))
         return body(query, *rest)
 
     return jax.shard_map(run, mesh=mesh, in_specs=in_specs, out_specs=out_specs, check_vma=False)

time: 70.3 us -> 64.4 us (0.916)
  local copies, waits for them, and re-layouts: 4.5 us -> 0 us
  Pallas kernels: 64.9 us -> 63.6 us
    unnamed x10 -> x0, local copies, waits for them, and re-layouts: 4.5 us -> none
    pallas_call x1, Pallas kernels: 64.9 us -> 61.6 us  [fused(): pl.pallas_call(functools.partial(fused_kernel, groups, columns), out_shap...]
    pallas_call x0 -> x1, Pallas kernels: none -> 1.97 us  [relay(): pl.pallas_call(relay_kernel, out_shape=[jax.ShapeDtypeStruct(a.shape, a.d...]
where the time goes in v1:
time: 64.4 us; the launch traced here: 64.2 us
  Pallas kernels  63.6 us (99%)
    pallas_call x1, Pallas kernels, fused(): pl.pallas_call(functools.partial(fused_kernel, groups, columns), out_shap...  61.6 us
    pallas_call x1, Pallas kernels, relay(): pl.pallas_call(relay_kernel, out_shape=[jax.ShapeDtypeStruct(a.shape, a.d...  1.97 us

profile of v1, /device:TPU:0, one launch (start us, length us, event | category | flops | bytes accessed | tf_op | source)
XLA Modules:
  0.0 64.2 jit_solution(18114144508740191309)
XLA Ops:
  0.6 61.6 %shard_map.84 = (bf16[128,1024]{1,0:T(8,128)(2,1)}, bf16[128,1024]{1,0:T(8,128)(2,1)}, bf16[128,1024]{1,0:T(8,128)(2,1)}, bf16[128,1024]{1,0:T(8,128)(2,1)}) custom-call(s32[2]{0:T(128)} %global_ref.1, bf16[128,1024]{1,0:T(8,128)(2,1)} %q_ref.1, bf16[128,1024]{1,0:T(8,128)(2,1)} %k_ref.1, bf16[128,1024]{1,0:T(8,128)(2,1)} %v_ref.1, bf16[128,1024]{1,0:T(8,128)(2,1)} %g_ref.1), custom_call_target="tpu_custom_call" | custom-call | tf_op jit(solution)/shard_map/pallas_call | solution.py:540
  62.2 2.0 %shard_map.85 = (bf16[128,1024]{1,0:T(8,128)(2,1)}, bf16[128,1024]{1,0:T(8,128)(2,1)}, bf16[128,1024]{1,0:T(8,128)(2,1)}, bf16[128,1024]{1,0:T(8,128)(2,1)}) custom-call(bf16[128,1024]{1,0:T(8,128)(2,1)} %get-tuple-element.8.refs_0_, bf16[128,1024]{1,0:T(8,128)(2,1)} %get-tuple-element.9.refs_1_, bf16[128,1024]{1,0:T(8,128)(2,1)} %get-tuple-element.10.refs_2_, ...), custom_call_target="tpu_custom_call" | custom-call | tf_op jit(solution)/shard_map/pallas_call | solution.py:575

commit v2 on v1

--- a/solution.py
+++ b/solution.py
@@ -273,7 +273,7 @@
         refs, buf = (((k_ref, v_ref), kv), ((q_ref, g_ref), qg))[kind]
         for d in range(1, groups):
             target = lax.rem(h + d, groups)
-            arrival = qg_recv.at[pair] if kind else kv_recv.at[pair, d - 1]
+            arrival = (kv_recv, qg_recv)[kind].at[pair, d - 1]
             for a, ref in enumerate(refs):
                 remote(
                     ref.at[:, lanes_of(target, pair)], buf.at[pair, a, h],
@@ -288,14 +288,19 @@
                 side_send.at[0], side_recv.at[pair], (h, to),
             ).start()
 
-    def forward(pair, then=None):
+    def forward(pair, between, held=()):
         settle(kv.at[pair, :, h], own_sem.at[0, pair])
-        send_sides(pair, 0)
+        if 0 not in held:
+            send_sides(pair, 0)
         for d in range(1, groups):
             settle(kv.at[pair, :, lax.rem(h + groups - d, groups)], kv_recv.at[pair, d - 1])
+            if d not in held:
+                send_sides(pair, d)
+            if d in between:
+                between[d]()
+        offer(pair)
+        for d in held:
             send_sides(pair, d)
-            if d == 1 and then is not None:
-                send_in(*then)
 
     seg_of = [lax.div(global_ref[w], columns) for w in range(GLOBALS)]
     col_of = [lax.rem(global_ref[w], columns) for w in range(GLOBALS)]
@@ -360,11 +365,10 @@
                     buf.at[pair, h], ref.at[:, lanes_of(h, pair)], keep_sem.at[0]
                 ).start()
 
-    def send_dsides(pair, j):
-        steps = pl.ds(2 * j, 2)
+    def send_dsides(pair, i):
         for way, to in ((0, left), (1, right)):
             remote(
-                dside.at[pair, way, :, steps], dside_in.at[pair, way, :, steps],
+                dside.at[pair, way, :, i], dside_in.at[pair, way, :, i],
                 ds_send.at[0], ds_recv.at[pair], (h, to),
             ).start()
 
@@ -413,26 +417,27 @@
         dq_out[pair, segment] = picked(d_query).astype(BF16)
         return d_key, d_value
 
-    def halves(pair, j):
-        both = [unit(pair, i) for i in (2 * j, 2 * j + 1)]
-        for a in range(2):
-            summed = both[0][a][:dense] + both[1][a][:dense]
-            if j == 0:
-                dsum[pair, a] = summed
-            else:
-                dsum[pair, a] += summed
-            for i in range(2):
-                dside[pair, 0, a, 2 * j + i] = both[i][a][dense : dense + rows].astype(BF16)
-                dside[pair, 1, a, 2 * j + i] = both[i][a][dense + rows :].astype(BF16)
-        send_dsides(pair, j)
-        for i in (2 * j, 2 * j + 1):
-            send_out(pair, i, 0)
-
-    def arrive(pair):
-        settle(qg.at[pair, :, h], own_sem.at[1, pair])
-        settle(qg.at[pair, :, pl.ds(0, groups - 1)], qg_recv.at[pair])
+    def ready(pair):
         settle(side.at[pair], side_recv.at[pair])
         settle(glob.at[pair, :, pl.ds(0, rows - strip)], gb_recv.at[pair])
+        settle(qg.at[pair, :, h], own_sem.at[1, pair])
+
+    def run(pair, i, closing=False):
+        segment = lax.rem(h + i + 1, groups)
+        if i < groups - 1:
+            settle(qg.at[pair, :, segment], qg_recv.at[pair, groups - 2 - i])
+        grads = unit(pair, i)
+        for a in range(2):
+            if i == groups - 1:
+                dsum[pair, a] = grads[a][:dense]
+            else:
+                dsum[pair, a] += grads[a][:dense]
+            dside[pair, 0, a, i] = grads[a][dense : dense + rows].astype(BF16)
+            dside[pair, 1, a, i] = grads[a][dense + rows :].astype(BF16)
+        if closing:
+            scatter(pair)
+        send_dsides(pair, i)
+        send_out(pair, i, 0)
 
     def scatter(pair):
         for w in range(GLOBALS):
@@ -478,25 +483,29 @@
                 buf[pair, segment] = whole.astype(BF16)
             send_out(pair, i, 2)
 
+    def then(step, *rest):
+        return functools.partial(step, *rest)
+
     send_in(0, 0)
-    for pair in range(pairs):
-        if pair + 1 < pairs:
-            send_in(0, pair + 1)
-        forward(pair, (1, pair))
-        offer(pair)
-    for pair in range(pairs):
-        choose(pair)
-    for pair in range(pairs):
-        arrive(pair)
-        halves(pair, 0)
-        if pair:
-            gather(pair - 1)
-        halves(pair, 1)
-        scatter(pair)
-        if pair:
-            finish(pair - 1)
-    gather(pairs - 1)
-    finish(pairs - 1)
+    forward(0, {2: then(send_in, 0, 1)}, (2, 3))
+    send_in(1, 0)
+    choose(0)
+    forward(1, {1: then(send_in, 1, 1)}, range(groups))
+    ready(0)
+    run(0, 3)
+    run(0, 2)
+    choose(1)
+    run(0, 1)
+    run(0, 0, True)
+    ready(1)
+    run(1, 3)
+    run(1, 2)
+    gather(0)
+    run(1, 1)
+    run(1, 0, True)
+    finish(0)
+    gather(1)
+    finish(1)
 
     shares = pl.ds(0, groups - 1)
     for n in range(2):
@@ -534,7 +543,7 @@
         half((pairs, columns, 2 * GLOBALS, strip, LANES)),
         half((pairs, 2 * GLOBALS, *tile)),
     ] + [half((pairs, groups, *tile))] * 4
-    scratch += [dma((2, pairs)), dma((pairs, groups - 1))] + [dma((pairs,))] * 7
+    scratch += [dma((2, pairs))] + [dma((pairs, groups - 1))] * 2 + [dma((pairs,))] * 6
     scratch += [dma((2,)), dma((1,)), dma((4,)), dma((1,)), dma((2,)), dma((2,)), dma((1,))]
     hbm = pl.BlockSpec(memory_space=pltpu.HBM)
     return pl.pallas_call(
@@ -605,7 +614,7 @@
     def run(query, *rest):
         rows, width = query.shape
         whole_column = rows == BLOCK and groups - 1 == RANDOMS and groups % 2 == 0
-        if whole_column and rows % (16 * columns) == 0 and width % (groups * LANES) == 0:
+        if whole_column and rows % (16 * columns) == 0 and width == 2 * groups * LANES:
             return relay(*fused(groups, columns, query, *rest))
         return body(query, *rest)
 

time: 64.4 us -> 59.8 us (0.929)
  Pallas kernels: 63.6 us -> 59 us
    pallas_call x1, Pallas kernels: 61.6 us -> 57 us  [fused(): pl.pallas_call(functools.partial(fused_kernel, groups, columns), out_shap...]
where the time goes in v2:
time: 59.8 us; the launch traced here: 59.6 us
  Pallas kernels  59 us (99%)
  between operations  0.64 us (1%)
    pallas_call x1, Pallas kernels, fused(): pl.pallas_call(functools.partial(fused_kernel, groups, columns), out_shap...  57 us
    pallas_call x1, Pallas kernels, relay(): pl.pallas_call(relay_kernel, out_shape=[jax.ShapeDtypeStruct(a.shape, a.d...  1.97 us

profile of v2, /device:TPU:0, one launch (start us, length us, event | category | flops | bytes accessed | tf_op | source)
XLA Modules:
  0.0 59.6 jit_solution(16489306848657284831)
XLA Ops:
  0.6 57.0 %shard_map.84 = (bf16[128,1024]{1,0:T(8,128)(2,1)}, bf16[128,1024]{1,0:T(8,128)(2,1)}, bf16[128,1024]{1,0:T(8,128)(2,1)}, bf16[128,1024]{1,0:T(8,128)(2,1)}) custom-call(s32[2]{0:T(128)} %global_ref.1, bf16[128,1024]{1,0:T(8,128)(2,1)} %q_ref.1, bf16[128,1024]{1,0:T(8,128)(2,1)} %k_ref.1, bf16[128,1024]{1,0:T(8,128)(2,1)} %v_ref.1, bf16[128,1024]{1,0:T(8,128)(2,1)} %g_ref.1), custom_call_target="tpu_custom_call" | custom-call | tf_op jit(solution)/shard_map/pallas_call | solution.py:549
  57.6 2.0 %shard_map.85 = (bf16[128,1024]{1,0:T(8,128)(2,1)}, bf16[128,1024]{1,0:T(8,128)(2,1)}, bf16[128,1024]{1,0:T(8,128)(2,1)}, bf16[128,1024]{1,0:T(8,128)(2,1)}) custom-call(bf16[128,1024]{1,0:T(8,128)(2,1)} %get-tuple-element.8.refs_0_, bf16[128,1024]{1,0:T(8,128)(2,1)} %get-tuple-element.9.refs_1_, bf16[128,1024]{1,0:T(8,128)(2,1)} %get-tuple-element.10.refs_2_, ...), custom_call_target="tpu_custom_call" | custom-call | tf_op jit(solution)/shard_map/pallas_call | solution.py:584

commit v3 on v2

--- a/solution.py
+++ b/solution.py
@@ -422,7 +422,7 @@
         settle(glob.at[pair, :, pl.ds(0, rows - strip)], gb_recv.at[pair])
         settle(qg.at[pair, :, h], own_sem.at[1, pair])
 
-    def run(pair, i, closing=False):
+    def run(pair, i, closing=False, share_now=True):
         segment = lax.rem(h + i + 1, groups)
         if i < groups - 1:
             settle(qg.at[pair, :, segment], qg_recv.at[pair, groups - 2 - i])
@@ -436,7 +436,8 @@
             dside[pair, 1, a, i] = grads[a][dense + rows :].astype(BF16)
         if closing:
             scatter(pair)
-        send_dsides(pair, i)
+        if share_now:
+            send_dsides(pair, i)
         send_out(pair, i, 0)
 
     def scatter(pair):
@@ -492,17 +493,25 @@
     choose(0)
     forward(1, {1: then(send_in, 1, 1)}, range(groups))
     ready(0)
-    run(0, 3)
-    run(0, 2)
+    run(0, 3, False, False)
     choose(1)
-    run(0, 1)
-    run(0, 0, True)
+    run(0, 2, False, False)
+    send_dsides(0, 3)
+    run(0, 1, False, False)
+    send_dsides(0, 2)
+    run(0, 0, True, False)
     ready(1)
-    run(1, 3)
-    run(1, 2)
+    send_dsides(0, 1)
+    run(1, 3, False, False)
+    send_dsides(0, 0)
+    run(1, 2, False, False)
     gather(0)
-    run(1, 1)
-    run(1, 0, True)
+    send_dsides(1, 3)
+    run(1, 1, False, False)
+    send_dsides(1, 2)
+    run(1, 0, True, False)
+    send_dsides(1, 1)
+    send_dsides(1, 0)
     finish(0)
     gather(1)
     finish(1)

time: 59.8 us -> 57.9 us (0.968)
  Pallas kernels: 59 us -> 57.1 us
    pallas_call x1, Pallas kernels: 57 us -> 55.1 us  [fused(): pl.pallas_call(functools.partial(fused_kernel, groups, columns), out_shap...]
where the time goes in v3:
time: 57.9 us; the launch traced here: 57.7 us
  Pallas kernels  57.1 us (99%)
  between operations  0.64 us (1%)
    pallas_call x1, Pallas kernels, fused(): pl.pallas_call(functools.partial(fused_kernel, groups, columns), out_shap...  55.1 us
    pallas_call x1, Pallas kernels, relay(): pl.pallas_call(relay_kernel, out_shape=[jax.ShapeDtypeStruct(a.shape, a.d...  1.97 us

profile of v3, /device:TPU:0, one launch (start us, length us, event | category | flops | bytes accessed | tf_op | source)
XLA Modules:
  0.0 57.7 jit_solution(17374633987946479751)
XLA Ops:
  0.6 55.1 %shard_map.84 = (bf16[128,1024]{1,0:T(8,128)(2,1)}, bf16[128,1024]{1,0:T(8,128)(2,1)}, bf16[128,1024]{1,0:T(8,128)(2,1)}, bf16[128,1024]{1,0:T(8,128)(2,1)}) custom-call(s32[2]{0:T(128)} %global_ref.1, bf16[128,1024]{1,0:T(8,128)(2,1)} %q_ref.1, bf16[128,1024]{1,0:T(8,128)(2,1)} %k_ref.1, bf16[128,1024]{1,0:T(8,128)(2,1)} %v_ref.1, bf16[128,1024]{1,0:T(8,128)(2,1)} %g_ref.1), custom_call_target="tpu_custom_call" | custom-call | tf_op jit(solution)/shard_map/pallas_call | solution.py:558
  55.7 2.0 %shard_map.85 = (bf16[128,1024]{1,0:T(8,128)(2,1)}, bf16[128,1024]{1,0:T(8,128)(2,1)}, bf16[128,1024]{1,0:T(8,128)(2,1)}, bf16[128,1024]{1,0:T(8,128)(2,1)}) custom-call(bf16[128,1024]{1,0:T(8,128)(2,1)} %get-tuple-element.8.refs_0_, bf16[128,1024]{1,0:T(8,128)(2,1)} %get-tuple-element.9.refs_1_, bf16[128,1024]{1,0:T(8,128)(2,1)} %get-tuple-element.10.refs_2_, ...), custom_call_target="tpu_custom_call" | custom-call | tf_op jit(solution)/shard_map/pallas_call | solution.py:593

commit v4 on v3

--- a/solution.py
+++ b/solution.py
@@ -219,7 +219,8 @@
     qg, kv, side, cand, piece, glob, dsum, dside, dside_in, dg_out, dg_in, dg_sum,
     att_out, dq_out, dk_out, dv_out,
     own_sem, kv_recv, qg_recv, side_recv, ga_recv, gb_recv, ds_recv, da_recv, db_recv,
-    in_send, side_send, glob_send, ds_send, out_send, out_recv, keep_sem,
+    gs_recv, dt_recv, in_send, side_send, glob_send, ds_send, out_send, out_recv,
+    keep_sem, fixed_send,
 ):
     h = lax.axis_index("grp")
     c = lax.axis_index("seq")
@@ -302,16 +303,18 @@
         for d in held:
             send_sides(pair, d)
 
-    seg_of = [lax.div(global_ref[w], columns) for w in range(GLOBALS)]
-    col_of = [lax.rem(global_ref[w], columns) for w in range(GLOBALS)]
+    last = groups * columns - 1
+    other = global_ref[0] + global_ref[1] - last
+    seg_of = lax.div(other, columns)
+    col_of = lax.rem(other, columns)
+    moving, fixed = pl.ds(0, 2), pl.ds(2, 2)
 
     def offer(pair):
-        for w in range(GLOBALS):
-            for a in range(2):
-                chosen = kv[pair, a, 0]
-                for t in range(1, groups):
-                    chosen = jnp.where(seg_of[w] == t, kv[pair, a, t], chosen)
-                cand[pair, 2 * w + a] = chosen
+        for a in range(2):
+            chosen = kv[pair, a, 0]
+            for t in range(1, groups):
+                chosen = jnp.where(seg_of == t, kv[pair, a, t], chosen)
+            cand[pair, a] = chosen
         for e in range(1, columns):
             to = lax.rem(c + e, columns)
             remote(
@@ -320,14 +323,29 @@
             ).start()
         piece[pair, c] = cand[pair, :, rows_of(c), :]
 
+        @pl.when(c == columns - 1)
+        def _():
+            for to in range(columns - 1):
+                remote(
+                    kv.at[pair, :, groups - 1, rows_of(to), :],
+                    glob.at[pair, fixed, rows_of(to), :],
+                    fixed_send.at[0], gs_recv.at[pair], (h, to),
+                ).start()
+            for a in range(2):
+                glob[pair, 2 + a, rows_of(c), :] = kv[pair, a, groups - 1, rows_of(c), :]
+
     def choose(pair):
         settle(piece.at[pair, pl.ds(0, columns - 1)], ga_recv.at[pair])
-        for w in range(GLOBALS):
-            for a in range(2):
-                chosen = piece[pair, 0, 2 * w + a]
-                for e in range(1, columns):
-                    chosen = jnp.where(col_of[w] == e, piece[pair, e, 2 * w + a], chosen)
-                glob[pair, 2 * w + a, rows_of(c), :] = chosen
+        for a in range(2):
+            chosen = piece[pair, 0, a]
+            for e in range(1, columns):
+                chosen = jnp.where(col_of == e, piece[pair, e, a], chosen)
+            glob[pair, a, rows_of(c), :] = chosen
+
+        @pl.when(c < columns - 1)
+        def _():
+            settle(glob.at[pair, fixed, rows_of(c), :], gs_recv.at[pair])
+
         for e in range(1, columns):
             to = lax.rem(c + e, columns)
             remote(
@@ -337,7 +355,6 @@
 
     lane = lax.broadcasted_iota(jnp.int32, (rows, LANES), 1)
     factor = 1.0 / math.sqrt(HEAD_DIM)
-    last = groups * columns - 1
 
     def stacked(block):
         zero = jnp.zeros_like(block)
@@ -462,25 +479,39 @@
         for e in range(1, columns):
             to = lax.rem(c + e, columns)
             remote(
-                dg_sum.at[pair, :, rows_of(c), :], dg_sum.at[pair, :, rows_of(c), :],
+                dg_sum.at[pair, moving, rows_of(c), :], dg_sum.at[pair, moving, rows_of(c), :],
                 glob_send.at[3], db_recv.at[pair], (h, to),
             ).start()
 
+        @pl.when(c < columns - 1)
+        def _():
+            remote(
+                dg_sum.at[pair, fixed, rows_of(c), :], dg_sum.at[pair, fixed, rows_of(c), :],
+                fixed_send.at[1], dt_recv.at[pair], (h, columns - 1),
+            ).start()
+
     def finish(pair):
         settle(dside_in.at[pair], ds_recv.at[pair])
-        settle(dg_sum.at[pair, :, pl.ds(0, rows - strip)], db_recv.at[pair])
+        settle(dg_sum.at[pair, moving, pl.ds(0, rows - strip)], db_recv.at[pair])
+
+        @pl.when(c == columns - 1)
+        def _():
+            settle(dg_sum.at[pair, fixed, pl.ds(0, rows - strip)], dt_recv.at[pair])
+            span = pl.ds((groups - 1) * rows, rows)
+            for a in range(2):
+                dsum[pair, a, span] += dg_sum[pair, 2 + a].astype(F32)
+
         for i in range(groups):
             segment = lax.rem(h + i + 1, groups)
             low = lax.rem(i + at_last, groups)
             high = lax.rem(i + groups - at_first, groups)
             span = pl.ds(pl.multiple_of(segment * rows, rows), rows)
+            mine = (other == segment * columns + c).astype(F32)
             for a, buf in enumerate((dk_out, dv_out)):
                 whole = dsum[pair, a, span]
                 whole += dside_in[pair, 0, a, low].astype(F32)
                 whole += dside_in[pair, 1, a, high].astype(F32)
-                for w in range(GLOBALS):
-                    mine = (global_ref[w] == segment * columns + c).astype(F32)
-                    whole += dg_sum[pair, 2 * w + a].astype(F32) * mine
+                whole += dg_sum[pair, a].astype(F32) * mine
                 buf[pair, segment] = whole.astype(BF16)
             send_out(pair, i, 2)
 
@@ -523,9 +554,19 @@
         settle(kv.at[:, :, shares], out_recv.at[n])
     settle(side, side_send.at[0])
     settle(dside, ds_send.at[0])
-    for n in range(2):
-        settle(piece.at[:, pl.ds(0, columns - 1)], glob_send.at[2 * n])
-        settle(glob.at[:, :, pl.ds(0, rows - strip)], glob_send.at[2 * n + 1])
+    settle(piece.at[:, pl.ds(0, columns - 1)], glob_send.at[0])
+    settle(glob.at[:, :, pl.ds(0, rows - strip)], glob_send.at[1])
+    settle(dg_in.at[:, pl.ds(0, columns - 1)], glob_send.at[2])
+    settle(dg_sum.at[:, moving, pl.ds(0, rows - strip)], glob_send.at[3])
+
+    @pl.when(c == columns - 1)
+    def _():
+        settle(glob.at[:, fixed, pl.ds(0, rows - strip)], fixed_send.at[0])
+
+    @pl.when(c < columns - 1)
+    def _():
+        settle(glob.at[:, fixed, pl.ds(0, strip)], fixed_send.at[1])
+
     settle(kv.at[:, :, pl.ds(0, 2)], keep_sem.at[0])
 
 
@@ -542,8 +583,8 @@
         half((pairs, 2, groups, *tile)),
         half((pairs, 2, groups, *tile)),
         half((pairs, 2, 2, groups, *tile)),
-        half((pairs, 2 * GLOBALS, *tile)),
-        half((pairs, columns, 2 * GLOBALS, strip, LANES)),
+        half((pairs, 2, *tile)),
+        half((pairs, columns, 2, strip, LANES)),
         half((pairs, 2 * GLOBALS, *tile)),
         full((pairs, 2, (groups + GLOBALS) * rows, LANES)),
         half((pairs, 2, 2, groups, *tile)),
@@ -552,8 +593,8 @@
         half((pairs, columns, 2 * GLOBALS, strip, LANES)),
         half((pairs, 2 * GLOBALS, *tile)),
     ] + [half((pairs, groups, *tile))] * 4
-    scratch += [dma((2, pairs))] + [dma((pairs, groups - 1))] * 2 + [dma((pairs,))] * 6
-    scratch += [dma((2,)), dma((1,)), dma((4,)), dma((1,)), dma((2,)), dma((2,)), dma((1,))]
+    scratch += [dma((2, pairs))] + [dma((pairs, groups - 1))] * 2 + [dma((pairs,))] * 8
+    scratch += [dma((2,)), dma((1,)), dma((4,)), dma((1,)), dma((2,)), dma((2,)), dma((1,)), dma((2,))]
     hbm = pl.BlockSpec(memory_space=pltpu.HBM)
     return pl.pallas_call(
         functools.partial(fused_kernel, groups, columns),

time: 57.9 us -> 56.9 us (0.983)
  Pallas kernels: 57.1 us -> 56 us
    pallas_call x1, Pallas kernels: 55.1 us -> 54 us  [fused(): pl.pallas_call(functools.partial(fused_kernel, groups, columns), out_shap...]
where the time goes in v4:
time: 56.9 us; the launch traced here: 56.6 us
  Pallas kernels  56 us (98%)
  between operations  0.64 us (1%)
    pallas_call x1, Pallas kernels, fused(): pl.pallas_call(functools.partial(fused_kernel, groups, columns), out_shap...  54 us
    pallas_call x1, Pallas kernels, relay(): pl.pallas_call(relay_kernel, out_shape=[jax.ShapeDtypeStruct(a.shape, a.d...  1.97 us

profile of v4, /device:TPU:0, one launch (start us, length us, event | category | flops | bytes accessed | tf_op | source)
XLA Modules:
  0.0 56.6 jit_solution(304791315045180079)
XLA Ops:
  0.6 54.0 %shard_map.84 = (bf16[128,1024]{1,0:T(8,128)(2,1)}, bf16[128,1024]{1,0:T(8,128)(2,1)}, bf16[128,1024]{1,0:T(8,128)(2,1)}, bf16[128,1024]{1,0:T(8,128)(2,1)}) custom-call(s32[2]{0:T(128)} %global_ref.1, bf16[128,1024]{1,0:T(8,128)(2,1)} %q_ref.1, bf16[128,1024]{1,0:T(8,128)(2,1)} %k_ref.1, bf16[128,1024]{1,0:T(8,128)(2,1)} %v_ref.1, bf16[128,1024]{1,0:T(8,128)(2,1)} %g_ref.1), custom_call_target="tpu_custom_call" | custom-call | tf_op jit(solution)/shard_map/pallas_call | solution.py:599
  54.7 2.0 %shard_map.85 = (bf16[128,1024]{1,0:T(8,128)(2,1)}, bf16[128,1024]{1,0:T(8,128)(2,1)}, bf16[128,1024]{1,0:T(8,128)(2,1)}, bf16[128,1024]{1,0:T(8,128)(2,1)}) custom-call(bf16[128,1024]{1,0:T(8,128)(2,1)} %get-tuple-element.8.refs_0_, bf16[128,1024]{1,0:T(8,128)(2,1)} %get-tuple-element.9.refs_1_, bf16[128,1024]{1,0:T(8,128)(2,1)} %get-tuple-element.10.refs_2_, ...), custom_call_target="tpu_custom_call" | custom-call | tf_op jit(solution)/shard_map/pallas_call | solution.py:634

commit v5 on v4

--- a/solution.py
+++ b/solution.py
@@ -215,9 +215,9 @@
 
 def fused_kernel(
     groups, columns, global_ref, q_ref, k_ref, v_ref, g_ref,
-    att_ref, dq_ref, dk_ref, dv_ref,
+    out_ref,
     qg, kv, side, cand, piece, glob, dsum, dside, dside_in, dg_out, dg_in, dg_sum,
-    att_out, dq_out, dk_out, dv_out,
+    row_parts, key_parts,
     own_sem, kv_recv, qg_recv, side_recv, ga_recv, gb_recv, ds_recv, da_recv, db_recv,
     gs_recv, dt_recv, in_send, side_send, glob_send, ds_send, out_send, out_recv,
     keep_sem, fixed_send,
@@ -367,20 +367,16 @@
             [wide[:HEAD_DIM, :rows], wide[HEAD_DIM:, rows:]], axis=0
         ).T
 
-    outgoing = ((att_out, att_ref), (dq_out, dq_ref), (dk_out, dk_ref), (dv_out, dv_ref))
-
-    def send_out(pair, i, first):
-        segment = lax.rem(h + i + 1, groups)
-        for buf, ref in outgoing[first : first + 2]:
-            if i < groups - 1:
-                remote(
-                    buf.at[pair, segment], ref.at[:, lanes_of(h, pair)],
-                    out_send.at[first // 2], out_recv.at[first // 2], (segment, c),
-                ).start()
-            else:
-                pltpu.make_async_copy(
-                    buf.at[pair, h], ref.at[:, lanes_of(h, pair)], keep_sem.at[0]
-                ).start()
+    def send_out(pair, segment, away, first):
+        buf = (row_parts, key_parts)[first // 2]
+        target = out_ref.at[pl.ds(first, 2), :, lanes_of(h, pair)]
+        if away:
+            remote(
+                buf.at[pair, segment], target,
+                out_send.at[first // 2], out_recv.at[first // 2], (segment, c),
+            ).start()
+        else:
+            pltpu.make_async_copy(buf.at[pair, h], target, keep_sem.at[0]).start()
 
     def send_dsides(pair, i):
         for way, to in ((0, left), (1, right)):
@@ -424,38 +420,63 @@
         prob = raised * (1.0 / jnp.sum(raised, axis=0, keepdims=True))
         half = prob.astype(BF16)
         d_prob = contract(value, grad, ((1,), (1,)))
-        result = contract(value, half, ((0,), (0,)))
         row_dot = jnp.sum(prob * d_prob, axis=0, keepdims=True)
         d_scores = (prob * (d_prob - row_dot)).astype(BF16)
-        d_query = contract(key, d_scores, ((0,), (0,))) * factor
-        d_value = contract(half, grad, ((1,), (0,)))
-        d_key = contract(d_scores, query, ((1,), (0,)))
-        att_out[pair, segment] = picked(result).astype(BF16)
-        dq_out[pair, segment] = picked(d_query).astype(BF16)
-        return d_key, d_value
+
+        def part(start, stop):
+            return (
+                contract(d_scores[start:stop], query, ((1,), (0,))),
+                contract(half[start:stop], grad, ((1,), (0,))),
+            )
+
+        def rows_out():
+            result = contract(value, half, ((0,), (0,)))
+            d_query = contract(key, d_scores, ((0,), (0,))) * factor
+            row_parts[pair, segment, 0] = picked(result).astype(BF16)
+            row_parts[pair, segment, 1] = picked(d_query).astype(BF16)
+
+        return part, rows_out
 
     def ready(pair):
         settle(side.at[pair], side_recv.at[pair])
         settle(glob.at[pair, :, pl.ds(0, rows - strip)], gb_recv.at[pair])
         settle(qg.at[pair, :, h], own_sem.at[1, pair])
 
-    def run(pair, i, closing=False, share_now=True):
+    def run(pair, i, closing=(), share_now=True):
         segment = lax.rem(h + i + 1, groups)
         if i < groups - 1:
             settle(qg.at[pair, :, segment], qg_recv.at[pair, groups - 2 - i])
-        grads = unit(pair, i)
-        for a in range(2):
-            if i == groups - 1:
-                dsum[pair, a] = grads[a][:dense]
-            else:
-                dsum[pair, a] += grads[a][:dense]
-            dside[pair, 0, a, i] = grads[a][dense : dense + rows].astype(BF16)
-            dside[pair, 1, a, i] = grads[a][dense + rows :].astype(BF16)
+        part, rows_out = unit(pair, i)
+
+        def summed(start, stop):
+            grads = part(start, stop)
+            for a in range(2):
+                if i == groups - 1:
+                    dsum[pair, a, start:stop] = grads[a]
+                else:
+                    dsum[pair, a, start:stop] += grads[a]
+
+        def sides_out():
+            grads = part(dense, dense + 2 * rows)
+            for a in range(2):
+                dside[pair, 0, a, i] = grads[a][:rows].astype(BF16)
+                dside[pair, 1, a, i] = grads[a][rows:].astype(BF16)
+
         if closing:
+            summed(groups * rows, dense)
             scatter(pair)
-        if share_now:
-            send_dsides(pair, i)
-        send_out(pair, i, 0)
+            sides_out()
+            for late in closing:
+                send_dsides(pair, late)
+            rows_out()
+            summed(0, groups * rows)
+        else:
+            rows_out()
+            summed(0, dense)
+            sides_out()
+            if share_now:
+                send_dsides(pair, i)
+        send_out(pair, segment, i < groups - 1, 0)
 
     def scatter(pair):
         for w in range(GLOBALS):
@@ -501,19 +522,20 @@
             for a in range(2):
                 dsum[pair, a, span] += dg_sum[pair, 2 + a].astype(F32)
 
-        for i in range(groups):
-            segment = lax.rem(h + i + 1, groups)
-            low = lax.rem(i + at_last, groups)
-            high = lax.rem(i + groups - at_first, groups)
+        for n in range(groups):
+            segment = n + jnp.where(h <= n, 1, 0) if n < groups - 1 else h
+            place = lax.rem(segment + 2 * groups - 1 - h, groups)
+            low = lax.rem(place + at_last, groups)
+            high = lax.rem(place + groups - at_first, groups)
             span = pl.ds(pl.multiple_of(segment * rows, rows), rows)
             mine = (other == segment * columns + c).astype(F32)
-            for a, buf in enumerate((dk_out, dv_out)):
+            for a in range(2):
                 whole = dsum[pair, a, span]
                 whole += dside_in[pair, 0, a, low].astype(F32)
                 whole += dside_in[pair, 1, a, high].astype(F32)
                 whole += dg_sum[pair, a].astype(F32) * mine
-                buf[pair, segment] = whole.astype(BF16)
-            send_out(pair, i, 2)
+                key_parts[pair, segment, a] = whole.astype(BF16)
+            send_out(pair, segment, n < groups - 1, 2)
 
     def then(step, *rest):
         return functools.partial(step, *rest)
@@ -530,9 +552,8 @@
     send_dsides(0, 3)
     run(0, 1, False, False)
     send_dsides(0, 2)
-    run(0, 0, True, False)
+    run(0, 0, (1,))
     ready(1)
-    send_dsides(0, 1)
     run(1, 3, False, False)
     send_dsides(0, 0)
     run(1, 2, False, False)
@@ -540,9 +561,7 @@
     send_dsides(1, 3)
     run(1, 1, False, False)
     send_dsides(1, 2)
-    run(1, 0, True, False)
-    send_dsides(1, 1)
-    send_dsides(1, 0)
+    run(1, 0, (1, 0))
     finish(0)
     gather(1)
     finish(1)
@@ -592,15 +611,15 @@
         half((pairs, 2 * GLOBALS, *tile)),
         half((pairs, columns, 2 * GLOBALS, strip, LANES)),
         half((pairs, 2 * GLOBALS, *tile)),
-    ] + [half((pairs, groups, *tile))] * 4
+    ] + [half((pairs, groups, 2, *tile))] * 2
     scratch += [dma((2, pairs))] + [dma((pairs, groups - 1))] * 2 + [dma((pairs,))] * 8
     scratch += [dma((2,)), dma((1,)), dma((4,)), dma((1,)), dma((2,)), dma((2,)), dma((1,)), dma((2,))]
     hbm = pl.BlockSpec(memory_space=pltpu.HBM)
     return pl.pallas_call(
         functools.partial(fused_kernel, groups, columns),
-        out_shape=[jax.ShapeDtypeStruct((rows, width), BF16)] * 4,
+        out_shape=jax.ShapeDtypeStruct((4, rows, width), BF16),
         in_specs=[pl.BlockSpec(memory_space=pltpu.SMEM)] + [hbm] * 4,
-        out_specs=[hbm] * 4,
+        out_specs=hbm,
         scratch_shapes=scratch,
         compiler_params=pltpu.CompilerParams(
             collective_id=0, has_side_effects=True, vmem_limit_bytes=63 * 2**20
@@ -611,37 +630,37 @@
 CHUNKS = 4
 
 
-def relay_kernel(*refs):
-    count = (len(refs) - 3) // 2
-    sources, targets = refs[:count], refs[count : 2 * count]
-    held, in_sem, out_sem = refs[2 * count :]
+def relay_kernel(source, *refs):
+    targets, (held, in_sem, out_sem) = refs[:-3], refs[-3:]
     rows = held.shape[1] // CHUNKS
-    for part in range(CHUNKS):
-        at = pl.ds(part * rows, rows)
-        for n in range(count):
-            pltpu.make_async_copy(sources[n].at[at], held.at[n, at], in_sem.at[part]).start()
-    for part in range(CHUNKS):
-        at = pl.ds(part * rows, rows)
-        pltpu.make_async_copy(held.at[:, at], held.at[:, at], in_sem.at[part]).wait()
-        for n in range(count):
-            pltpu.make_async_copy(held.at[n, at], targets[n].at[at], out_sem.at[0]).start()
+    parts = [pl.ds(part * rows, rows) for part in range(CHUNKS)]
+    arrivals = [
+        pltpu.make_async_copy(source.at[:, at], held.at[:, at], in_sem.at[part])
+        for part, at in enumerate(parts)
+    ]
+    for copy in arrivals:
+        copy.start()
+    for copy, at in zip(arrivals, parts):
+        copy.wait()
+        for n, target in enumerate(targets):
+            pltpu.make_async_copy(held.at[n, at], target.at[at], out_sem.at[0]).start()
     pltpu.make_async_copy(held, held, out_sem.at[0]).wait()
 
 
-def relay(*arrays):
+def relay(stacked):
     hbm = pl.BlockSpec(memory_space=pltpu.HBM)
-    count = len(arrays)
+    count, *shape = stacked.shape
     return pl.pallas_call(
         relay_kernel,
-        out_shape=[jax.ShapeDtypeStruct(a.shape, a.dtype) for a in arrays],
-        in_specs=[hbm] * count,
+        out_shape=[jax.ShapeDtypeStruct(tuple(shape), stacked.dtype)] * count,
+        in_specs=[hbm],
         out_specs=[hbm] * count,
         scratch_shapes=[
-            pltpu.VMEM((count, *arrays[0].shape), arrays[0].dtype),
+            pltpu.VMEM(stacked.shape, stacked.dtype),
             pltpu.SemaphoreType.DMA((CHUNKS,)),
             pltpu.SemaphoreType.DMA((1,)),
         ],
-    )(*arrays)
+    )(stacked)
 
 
 def solution(mesh):
@@ -665,7 +684,7 @@
         rows, width = query.shape
         whole_column = rows == BLOCK and groups - 1 == RANDOMS and groups % 2 == 0
         if whole_column and rows % (16 * columns) == 0 and width == 2 * groups * LANES:
-            return relay(*fused(groups, columns, query, *rest))
+            return relay(fused(groups, columns, query, *rest))
         return body(query, *rest)
 
     return jax.shard_map(run, mesh=mesh, in_specs=in_specs, out_specs=out_specs, check_vma=False)

time: 56.9 us -> 56.6 us (level)
  no operation moved by 1% of the time
where the time goes in v5:
time: 56.6 us; the launch traced here: 56.4 us
  Pallas kernels  55.8 us (99%)
  between operations  0.64 us (1%)
    pallas_call x1, Pallas kernels, fused(): pl.pallas_call(functools.partial(fused_kernel, groups, columns), out_shap...  53.8 us
    pallas_call x1, Pallas kernels, relay(): pl.pallas_call(relay_kernel, out_shape=[jax.ShapeDtypeStruct(tuple(shape)...  1.94 us

profile of v5, /device:TPU:0, one launch (start us, length us, event | category | flops | bytes accessed | tf_op | source)
XLA Modules:
  0.0 56.4 jit_solution(9408735808818818353)
XLA Ops:
  0.6 53.8 %shard_map.84.source = bf16[4,128,1024]{2,1,0:T(8,128)(2,1)} custom-call(s32[2]{0:T(128)} %global_ref.1, bf16[128,1024]{1,0:T(8,128)(2,1)} %q_ref.1, bf16[128,1024]{1,0:T(8,128)(2,1)} %k_ref.1, bf16[128,1024]{1,0:T(8,128)(2,1)} %v_ref.1, bf16[128,1024]{1,0:T(8,128)(2,1)} %g_ref.1), custom_call_target="tpu_custom_call" | custom-call | tf_op jit(solution)/shard_map/pallas_call | solution.py:618
  54.5 1.9 %shard_map.85 = (bf16[128,1024]{1,0:T(8,128)(2,1)}, bf16[128,1024]{1,0:T(8,128)(2,1)}, bf16[128,1024]{1,0:T(8,128)(2,1)}, bf16[128,1024]{1,0:T(8,128)(2,1)}) custom-call(bf16[4,128,1024]{2,1,0:T(8,128)(2,1)} %shard_map.84.source), custom_call_target="tpu_custom_call" | custom-call | tf_op jit(solution)/shard_map/pallas_call | solution.py:653

commit v6 on v5

--- a/solution.py
+++ b/solution.py
@@ -469,14 +469,15 @@
             for late in closing:
                 send_dsides(pair, late)
             rows_out()
+            send_out(pair, segment, i < groups - 1, 0)
             summed(0, groups * rows)
         else:
             rows_out()
+            send_out(pair, segment, i < groups - 1, 0)
             summed(0, dense)
             sides_out()
             if share_now:
                 send_dsides(pair, i)
-        send_out(pair, segment, i < groups - 1, 0)
 
     def scatter(pair):
         for w in range(GLOBALS):

time: 56.6 us -> 56.6 us (level)
  no operation moved by 1% of the time
where the time goes in v6:
time: 56.6 us; the launch traced here: 56.4 us
  Pallas kernels  55.8 us (99%)
  between operations  0.64 us (1%)
    pallas_call x1, Pallas kernels, fused(): pl.pallas_call(functools.partial(fused_kernel, groups, columns), out_shap...  53.8 us
    pallas_call x1, Pallas kernels, relay(): pl.pallas_call(relay_kernel, out_shape=[jax.ShapeDtypeStruct(tuple(shape)...  1.94 us

profile of v6, /device:TPU:0, one launch (start us, length us, event | category | flops | bytes accessed | tf_op | source)
XLA Modules:
  0.0 56.4 jit_solution(9911942653763553368)
XLA Ops:
  0.6 53.8 %shard_map.84.source = bf16[4,128,1024]{2,1,0:T(8,128)(2,1)} custom-call(s32[2]{0:T(128)} %global_ref.1, bf16[128,1024]{1,0:T(8,128)(2,1)} %q_ref.1, bf16[128,1024]{1,0:T(8,128)(2,1)} %k_ref.1, bf16[128,1024]{1,0:T(8,128)(2,1)} %v_ref.1, bf16[128,1024]{1,0:T(8,128)(2,1)} %g_ref.1), custom_call_target="tpu_custom_call" | custom-call | tf_op jit(solution)/shard_map/pallas_call | solution.py:619
  54.5 1.9 %shard_map.85 = (bf16[128,1024]{1,0:T(8,128)(2,1)}, bf16[128,1024]{1,0:T(8,128)(2,1)}, bf16[128,1024]{1,0:T(8,128)(2,1)}, bf16[128,1024]{1,0:T(8,128)(2,1)}) custom-call(bf16[4,128,1024]{2,1,0:T(8,128)(2,1)} %shard_map.84.source), custom_call_target="tpu_custom_call" | custom-call | tf_op jit(solution)/shard_map/pallas_call | solution.py:654

commit v7 on v5

--- a/solution.py
+++ b/solution.py
@@ -557,9 +557,9 @@
     run(1, 3, False, False)
     send_dsides(0, 0)
     run(1, 2, False, False)
-    gather(0)
     send_dsides(1, 3)
     run(1, 1, False, False)
+    gather(0)
     send_dsides(1, 2)
     run(1, 0, (1, 0))
     finish(0)

time: 56.6 us -> 56.6 us (level)
  no operation moved by 1% of the time
where the time goes in v7:
time: 56.6 us; the launch traced here: 56.4 us
  Pallas kernels  55.7 us (98%)
  between operations  0.64 us (1%)
    pallas_call x1, Pallas kernels, fused(): pl.pallas_call(functools.partial(fused_kernel, groups, columns), out_shap...  53.8 us
    pallas_call x1, Pallas kernels, relay(): pl.pallas_call(relay_kernel, out_shape=[jax.ShapeDtypeStruct(tuple(shape)...  1.94 us

profile of v7, /device:TPU:0, one launch (start us, length us, event | category | flops | bytes accessed | tf_op | source)
XLA Modules:
  0.0 56.4 jit_solution(12171974563101458905)
XLA Ops:
  0.6 53.8 %shard_map.84.source = bf16[4,128,1024]{2,1,0:T(8,128)(2,1)} custom-call(s32[2]{0:T(128)} %global_ref.1, bf16[128,1024]{1,0:T(8,128)(2,1)} %q_ref.1, bf16[128,1024]{1,0:T(8,128)(2,1)} %k_ref.1, bf16[128,1024]{1,0:T(8,128)(2,1)} %v_ref.1, bf16[128,1024]{1,0:T(8,128)(2,1)} %g_ref.1), custom_call_target="tpu_custom_call" | custom-call | tf_op jit(solution)/shard_map/pallas_call | solution.py:618
  54.4 1.9 %shard_map.85 = (bf16[128,1024]{1,0:T(8,128)(2,1)}, bf16[128,1024]{1,0:T(8,128)(2,1)}, bf16[128,1024]{1,0:T(8,128)(2,1)}, bf16[128,1024]{1,0:T(8,128)(2,1)}) custom-call(bf16[4,128,1024]{2,1,0:T(8,128)(2,1)} %shard_map.84.source), custom_call_target="tpu_custom_call" | custom-call | tf_op jit(solution)/shard_map/pallas_call | solution.py:653
